TPU v7x, 256 devices: a whole 4x4x8 slice. The times are simulated.
256 devices in a mesh: pipe: 16 (over x, z_hi, core), expert: 16 (over y, z_lo).
Axes of the slice: x: 4, y: 4, z: 8 (z_hi: 2, z_lo: 4; z = z_hi * 4 + z_lo), core: 2. Of those that a mesh axis runs over, the one named last changes fastest.
Arguments:
- tokens: bfloat16 [16, 2048, 1440], P('pipe', 'expert'), may hold values from -6 to 6
- routes_fwd: int32 [16, 2048, 4], P('pipe', 'expert'), may hold values from 0 to 7, all different within a row; in each aligned block of 128 rows (0 to 127, 128 to 255, ..., all dimensions but the last counted through in order) at most 68 rows name the same one
- probs_fwd: float32 [16, 2048, 4], P('pipe', 'expert'), may hold values from 0.1 to 0.6
- grad_out: bfloat16 [16, 2048, 1440], P('pipe', 'expert'), may hold values from -6 to 6
- routes_bwd: int32 [16, 2048, 4], P('pipe', 'expert'), may hold values from 0 to 7, all different within a row; in each aligned block of 128 rows (0 to 127, 128 to 255, ..., all dimensions but the last counted through in order) at most 68 rows name the same one
- probs_bwd: float32 [16, 2048, 4], P('pipe', 'expert'), may hold values from 0.1 to 0.6
- w_in: bfloat16 [16, 16, 1440, 1440], P('pipe', 'expert'), may hold values from -0.15625 to 0.15625
- w_down: bfloat16 [16, 16, 720, 1440], P('pipe', 'expert'), may hold values from -0.15625 to 0.15625
- saved_codes: bfloat16 [16, 17408, 1440], P('pipe', 'expert'), may hold values from -6 to 6
- saved_scales: bfloat16 [16, 17408, 90], P('pipe', 'expert'), may hold values from 0.039794922 to 0.3984375
- saved_exponent: int32 [16, 16], P('pipe', 'expert'), may hold values from -2 to 1
Outputs:
- moe_out: bfloat16 [16, 2048, 1440], P('pipe', 'expert')
- grad_in: bfloat16 [16, 2048, 1440], P('pipe', 'expert')
Inputs may be any that keep to these rules, and one draw needn't show every extreme that they name: `routes_fwd`: each row names 4 different experts; over the rows of one device no expert is named more than 68 times, and in every draw some device names some expert exactly 68 times. `routes_bwd`: each row names 4 different experts; over the rows of one device no expert is named more than 68 times, and in every draw some device names some expert exactly 68 times.
All inputs are finite; a program needn't handle non-finite values.
Results may differ from a plain program's by a relative error of at most 0.0065.
Values may be sent and summed in bfloat16 or wider, within the bound.
A program may use at most 128 MiB of HBM per device.

v0:
```python
import jax
import jax.numpy as jnp
from jax import lax
from jax.sharding import PartitionSpec as P


def from_partner(block, axis, stride):
    count = lax.axis_size(axis)
    route = []
    for low in range(count):
        high = low | 1 << stride
        if high != low and high < count:
            route += [(low, high), (high, low)]
    return lax.ppermute(block, axis, route)


def power_two(exponent):
    running = jnp.zeros(exponent.shape, jnp.float32)
    for exponent_level in range(-2, 2):
        running = running + jnp.where(
            exponent == exponent_level, jnp.float32(2.0**exponent_level), jnp.float32(0.0)
        )
    return running


def send_rows(routes, row_data, experts, capacity):
    expert_ids = routes.reshape(-1)
    onehot = (expert_ids[:, None] == jnp.arange(experts, dtype=jnp.int32)[None, :]).astype(
        jnp.int32
    )
    before = jnp.cumsum(onehot, axis=0) - onehot
    slot_index = jnp.sum(before * onehot, axis=1)
    target = expert_ids * capacity + slot_index
    matches = jnp.arange(experts * capacity, dtype=jnp.int32)[:, None] == target[None, :]
    choosing = jnp.sum(
        matches.astype(jnp.bfloat16).reshape(experts * capacity, row_data.shape[0], -1), axis=2
    )
    copied = jnp.dot(choosing, row_data, preferred_element_type=jnp.float32)
    return (expert_ids, slot_index, matches, copied)


def expert_forward(inputs, weight_in, weight_down, unit_count):
    gate_up = jnp.dot(inputs, weight_in, preferred_element_type=jnp.float32)
    hidden = (jax.nn.silu(gate_up[:, :unit_count]) * gate_up[:, unit_count:]).astype(jnp.bfloat16)
    return jnp.dot(hidden, weight_down, preferred_element_type=jnp.float32).astype(jnp.bfloat16)


def expert_backward(
    grad_rows, saved_rows, block_rows, weight_in, weight_down, unit_count, block_size
):
    row_count = saved_rows.shape[0]
    values = (
        saved_rows.reshape(row_count, -1, block_size).astype(jnp.float32)
        * block_rows.astype(jnp.float32)[:, :, None]
    )
    values = values.reshape(row_count, 2 * unit_count)
    gate_part = values[:, :unit_count]
    up_part = values[:, unit_count:]
    hidden_grad = lax.dot_general(
        grad_rows, weight_down, (((1,), (1,)), ((), ())), preferred_element_type=jnp.float32
    )
    sigmoid_gate = jax.nn.sigmoid(gate_part)
    gate_grad = (
        hidden_grad * up_part * sigmoid_gate * (1.0 + gate_part * (1.0 - sigmoid_gate))
    ).astype(jnp.bfloat16)
    up_grad = (hidden_grad * gate_part * sigmoid_gate).astype(jnp.bfloat16)
    joined = jnp.concatenate([gate_grad, up_grad], axis=1)
    return lax.dot_general(
        joined, weight_in, (((1,), (1,)), ((), ())), preferred_element_type=jnp.float32
    ).astype(jnp.bfloat16)


def gather_pairs(returned, expert_ids, slot_index, capacity):
    table_rows = returned.reshape(-1, returned.shape[-1])
    even_rows = expert_ids * (2 * capacity) + slot_index
    first_half = jnp.take(table_rows, even_rows, axis=0).astype(jnp.float32)
    second = jnp.take(table_rows, even_rows + capacity, axis=0).astype(jnp.float32)
    return first_half + second


def local(
    tokens,
    routes_fwd,
    probs_fwd,
    grad_out,
    routes_bwd,
    probs_bwd,
    w_in,
    w_down,
    saved_codes,
    saved_scales,
    saved_exponent,
):
    devices = lax.axis_size("expert")
    experts = devices // 2
    row_count = saved_codes.shape[1]
    capacity = row_count // devices
    tok_count = tokens.shape[1]
    feature_count = tokens.shape[2]
    unit_count = w_down.shape[2]
    block_size = 2 * unit_count // saved_scales.shape[2]
    weight_in = w_in[0, 0]
    weight_down = w_down[0, 0]
    held_codes = saved_codes[0]
    held_scales = saved_scales[0] * power_two(saved_exponent[0, 0]).astype(jnp.bfloat16)
    mirror_codes = held_codes
    mirror_scales = held_scales
    for bit_number in range(lax.axis_size("pipe").bit_length() - 1):
        mirror_codes, mirror_scales = from_partner(
            (mirror_codes, mirror_scales), "pipe", bit_number
        )
    ids_now, slots_now, matches_now, copied_now = send_rows(
        routes_fwd[0], tokens[0], experts, capacity
    )
    send_now = copied_now.astype(jnp.bfloat16)
    ids_old, slots_old, matches_old, copied_old = send_rows(
        routes_bwd[0], grad_out[0], experts, capacity
    )
    slot_weight = jnp.sum(jnp.where(matches_old, probs_bwd[0].reshape(-1)[None, :], 0.0), axis=1)
    send_old = (copied_old * slot_weight[:, None]).astype(jnp.bfloat16)
    inputs_now, inputs_old = (
        lax.all_to_all(
            jnp.repeat(send_now.reshape(experts, capacity, feature_count), 2, axis=0),
            "expert",
            split_axis=0,
            concat_axis=0,
            tiled=True,
        ),
        lax.all_to_all(
            jnp.repeat(send_old.reshape(experts, capacity, feature_count), 2, axis=0),
            "expert",
            split_axis=0,
            concat_axis=0,
            tiled=True,
        ),
    )
    outputs = expert_forward(
        inputs_now.reshape(row_count, feature_count), weight_in, weight_down, unit_count
    )
    returned = lax.all_to_all(
        outputs.reshape(devices, capacity, feature_count),
        "expert",
        split_axis=0,
        concat_axis=0,
        tiled=True,
    )
    pairs = gather_pairs(returned, ids_now, slots_now, capacity)
    weighted = probs_fwd[0].reshape(-1, 1) * pairs
    moe_out = jnp.sum(weighted.reshape(tok_count, -1, feature_count), axis=1).astype(jnp.bfloat16)
    input_rows = expert_backward(
        inputs_old.reshape(row_count, feature_count),
        mirror_codes,
        mirror_scales,
        weight_in,
        weight_down,
        unit_count,
        block_size,
    )
    returned_grads = lax.all_to_all(
        input_rows.reshape(devices, capacity, feature_count),
        "expert",
        split_axis=0,
        concat_axis=0,
        tiled=True,
    )
    grad_pairs = gather_pairs(returned_grads, ids_old, slots_old, capacity)
    grad_in = jnp.sum(grad_pairs.reshape(tok_count, -1, feature_count), axis=1).astype(jnp.bfloat16)
    return (moe_out[None], grad_in[None])


def solution(mesh):
    in_specs = (
        P("pipe", "expert", None),
        P("pipe", "expert", None),
        P("pipe", "expert", None),
        P("pipe", "expert", None),
        P("pipe", "expert", None),
        P("pipe", "expert", None),
        P("pipe", "expert", None, None),
        P("pipe", "expert", None, None),
        P("pipe", "expert", None),
        P("pipe", "expert", None),
        P("pipe", "expert"),
    )
    out_specs = (P("pipe", "expert", None), P("pipe", "expert", None))
    return jax.shard_map(local, mesh=mesh, in_specs=in_specs, out_specs=out_specs, check_vma=False)
```

profile of v0, /device:TPU:26, one launch (start us, length us, event | category | flops | bytes accessed | tf_op | source)
XLA Modules:
  0.0 566.9 jit_solution(15689328979826501346)
XLA Ops:
  9.0 3.5 broadcast_in_dim.39
  12.5 8.9 %all-to-all-start = ((bf16[16,68,1440]{2,1,0:T(8,128)(2,1)}), bf16[16,68,1440]{2,1,0:T(8,128)(2,1)}, u32[]{:S(2)}, u32[]{:S(2)}) async-start(bf16[16,68,1440]{2,1,0:T(8,128)(2,1)} %bitcast.56), calls=%async_computation | async-start | bytes 7077888 | tf_op jit(solution)/shard_map/all_to_all | solution.py:122
  21.7 6.0 %collective-permute-done = bf16[1088,1440]{0,1:T(8,128)(2,1)} collective-permute-done((bf16[1088,1440]{0,1:T(8,128)(2,1)}, bf16[1088,1440]{0,1:T(8,128)(2,1)}, u32[]{:S(2)}, u32[]{:S(2)}) %collective-permute-start) | collective-permute-done | bytes 3133472 | tf_op jit(solution)/shard_map/ppermute | solution.py:14
  27.7 4.5 collective-permute-start.1
  39.0 206.1 %all-to-all-done = bf16[16,68,1440]{2,1,0:T(8,128)(2,1)} async-done(((bf16[16,68,1440]{2,1,0:T(8,128)(2,1)}), bf16[16,68,1440]{2,1,0:T(8,128)(2,1)}, u32[]{:S(2)}, u32[]{:S(2)}) %all-to-all-start) | async-done | bytes 3133472 | tf_op jit(solution)/shard_map/all_to_all | solution.py:122
  245.1 3.6 broadcast_in_dim.43
  248.7 6.4 %all-to-all-start.2 = ((bf16[16,68,1440]{2,1,0:T(8,128)(2,1)}), bf16[16,68,1440]{2,1,0:T(8,128)(2,1)}, u32[]{:S(2)}, u32[]{:S(2)}) async-start(bf16[16,68,1440]{2,1,0:T(8,128)(2,1)} %bitcast.57), calls=%async_computation.2 | async-start | bytes 7077888 | tf_op jit(solution)/shard_map/all_to_all | solution.py:129
  256.1 4.9 reshape.170
  261.0 9.9 %fusion.1 = f32[1088,1440]{0,1:T(8,128)S(1)} fusion(bf16[1088,1440]{1,0:T(8,128)(2,1)} %reshape.170, bf16[1,1,1440,1440]{3,2,1,0:T(8,128)(2,1)} %param.19), kind=kOutput, calls=%fused_computation.8 | convolution fusion | flops 4512153600 | bytes 13547520 | tf_op jit(solution)/shard_map/dot_general | solution.py:43
  270.9 57.4 %collective-permute-done.2 = bf16[1088,1440]{0,1:T(8,128)(2,1)} collective-permute-done((bf16[1088,1440]{0,1:T(8,128)(2,1)}, bf16[1088,1440]{0,1:T(8,128)(2,1)}, u32[]{:S(2)}, u32[]{:S(2)}) %collective-permute-start.2) | collective-permute-done | bytes 3133472 | tf_op jit(solution)/shard_map/ppermute | solution.py:14
  330.5 5.1 convolution_convert_fusion.1
  335.5 5.6 copy.44
  341.2 4.6 reshape.171
  345.8 7.6 %all-to-all-start.1 = ((bf16[16,68,1440]{2,1,0:T(8,128)(2,1)}), bf16[16,68,1440]{2,1,0:T(8,128)(2,1)}, u32[]{:S(2)}, u32[]{:S(2)}) async-start(bf16[16,68,1440]{2,1,0:T(8,128)(2,1)} %reshape.171), calls=%async_computation.1 | async-start | bytes 7077888 | tf_op jit(solution)/shard_map/all_to_all | solution.py:140
  355.7 4.4 collective-permute-start.5
  360.1 62.1 %collective-permute-done.5 = bf16[1088,90]{0,1:T(8,128)(2,1)S(1)} collective-permute-done((bf16[1088,90]{0,1:T(8,128)(2,1)S(1)}, bf16[1088,90]{0,1:T(8,128)(2,1)S(1)}, u32[]{:S(2)}, u32[]{:S(2)}) %collective-permute-start.5) | collective-permute-done | bytes 195872 | tf_op jit(solution)/shard_map/ppermute | solution.py:14
  423.7 6.7 %collective-permute-done.6 = bf16[1088,90]{0,1:T(8,128)(2,1)S(1)} collective-permute-done((bf16[1088,90]{0,1:T(8,128)(2,1)S(1)}, bf16[1088,90]{0,1:T(8,128)(2,1)S(1)}, u32[]{:S(2)}, u32[]{:S(2)}) %collective-permute-start.6) | collective-permute-done | bytes 195872 | tf_op jit(solution)/shard_map/ppermute | solution.py:14
  431.1 6.7 %collective-permute-done.7 = bf16[1088,90]{0,1:T(8,128)(2,1)S(1)} collective-permute-done((bf16[1088,90]{0,1:T(8,128)(2,1)S(1)}, bf16[1088,90]{0,1:T(8,128)(2,1)S(1)}, u32[]{:S(2)}, u32[]{:S(2)}) %collective-permute-start.7) | collective-permute-done | bytes 195872 | tf_op jit(solution)/shard_map/ppermute | solution.py:14
  437.8 4.9 reshape.177
  445.7 3.7 fusion.5
  449.4 7.3 %convolution_convert_fusion = bf16[1088,1440]{0,1:T(8,128)(2,1)} fusion(bf16[1,1,1440,1440]{3,2,1,0:T(8,128)(2,1)S(1)} %bitcast.61, bf16[1088,720]{0,1:T(8,128)(2,1)S(1)} %get-tuple-element.16, bf16[1088,720]{0,1:T(8,128)(2,1)S(1)} %get-tuple-element.15), kind=kOutput, calls=%fused_computation.4 | convolution fusion | flops 4519987200 | bytes 10414080 | tf_op jit(solution)/shard_map/dot_general | solution.py:68
  456.7 4.3 copy.50
  463.6 8.3 %all-to-all-start.3 = ((bf16[16,68,1440]{2,1,0:T(8,128)(2,1)}), bf16[16,68,1440]{2,1,0:T(8,128)(2,1)}, u32[]{:S(2)}, u32[]{:S(2)}) async-start(bf16[16,68,1440]{2,1,0:T(8,128)(2,1)} %reshape.178), calls=%async_computation.3 | async-start | bytes 7077888 | tf_op jit(solution)/shard_map/all_to_all | solution.py:159
  472.2 3.4 reshape.172
  475.7 3.0 gather_fusion
  486.3 3.8 reduce_sum.76
  491.1 52.4 %all-to-all-done.3 = bf16[16,68,1440]{2,1,0:T(8,128)(2,1)} async-done(((bf16[16,68,1440]{2,1,0:T(8,128)(2,1)}), bf16[16,68,1440]{2,1,0:T(8,128)(2,1)}, u32[]{:S(2)}, u32[]{:S(2)}) %all-to-all-start.3) | async-done | bytes 3133472 | tf_op jit(solution)/shard_map/all_to_all | solution.py:159
  543.4 3.4 reshape.179
  546.9 3.0 gather_fusion.2
  552.8 4.1 convert_add_fusion
  557.0 5.0 reshape.180
  562.0 3.8 reduce_sum.81
  (82 shorter events, 40.5 us)
Async XLA Ops:
  0.6 329.8 %copy-start = (bf16[1,1,720,1440]{3,2,1,0:T(8,128)(2,1)S(1)}, bf16[1,1,720,1440]{3,2,1,0:T(8,128)(2,1)}, u32[]{:S(2)}) copy-start(bf16[1,1,720,1440]{3,2,1,0:T(8,128)(2,1)} %param.20) | copy-start | bytes 6220804
  12.5 8.9 %copy-start.5 = (s32[1,128,4]{1,2,0:T(4,128)S(1)}, s32[1,128,4]{1,2,0:T(4,128)}, u32[]{:S(2)}) copy-start(s32[1,128,4]{1,2,0:T(4,128)} %param.17) | copy-start | bytes 6148
  12.5 21.2 %copy-start.6 = (f32[1,128,4]{1,2,0:T(4,128)S(1)}, f32[1,128,4]{1,2,0:T(4,128)}, u32[]{:S(2)}) copy-start(f32[1,128,4]{1,2,0:T(4,128)} %param.18) | copy-start | bytes 6148
  12.5 22.0 %copy-start.3 = (bf16[1,128,1440]{1,2,0:T(8,128)(2,1)S(1)}, bf16[1,128,1440]{1,2,0:T(8,128)(2,1)}, u32[]{:S(2)}) copy-start(bf16[1,128,1440]{1,2,0:T(8,128)(2,1)} %param.16) | copy-start | bytes 1105924
  12.5 232.6 %all-to-all-start = ((bf16[16,68,1440]{2,1,0:T(8,128)(2,1)}), bf16[16,68,1440]{2,1,0:T(8,128)(2,1)}, u32[]{:S(2)}, u32[]{:S(2)}) async-start(bf16[16,68,1440]{2,1,0:T(8,128)(2,1)} %bitcast.56), calls=%async_computation | async-start | bytes 7077888 | tf_op jit(solution)/shard_map/all_to_all | solution.py:122
  21.4 6.2 %collective-permute-start = (bf16[1088,1440]{0,1:T(8,128)(2,1)}, bf16[1088,1440]{0,1:T(8,128)(2,1)}, u32[]{:S(2)}, u32[]{:S(2)}) collective-permute-start(bf16[1088,1440]{0,1:T(8,128)(2,1)} %bitcast.62), channel_id=1, source_target_pairs={{0,16},{16,0},{32,48},{48,32},{64,80},{80,64},{96,112},{112,96},{1... | collective-permute-start | bytes 9400328 | tf_op jit(solution)/shard_map/ppermute | solution.py:14
  27.7 227.3 %collective-permute-start.1 = (bf16[1088,1440]{0,1:T(8,128)(2,1)}, bf16[1088,1440]{0,1:T(8,128)(2,1)}, u32[]{:S(2)}, u32[]{:S(2)}) collective-permute-start(bf16[1088,1440]{0,1:T(8,128)(2,1)} %collective-permute-done), channel_id=1, source_target_pairs={{0,32},{32,0},{16,48},{48,16},{64,96},{96,64},{80,112},{112,80},{1... | collective-permute-start | bytes 9400328 | tf_op jit(solution)/shard_map/ppermute | solution.py:14
  248.7 97.1 %all-to-all-start.2 = ((bf16[16,68,1440]{2,1,0:T(8,128)(2,1)}), bf16[16,68,1440]{2,1,0:T(8,128)(2,1)}, u32[]{:S(2)}, u32[]{:S(2)}) async-start(bf16[16,68,1440]{2,1,0:T(8,128)(2,1)} %bitcast.57), calls=%async_computation.2 | async-start | bytes 7077888 | tf_op jit(solution)/shard_map/all_to_all | solution.py:129
  255.0 73.3 %collective-permute-start.2 = (bf16[1088,1440]{0,1:T(8,128)(2,1)}, bf16[1088,1440]{0,1:T(8,128)(2,1)}, u32[]{:S(2)}, u32[]{:S(2)}) collective-permute-start(bf16[1088,1440]{0,1:T(8,128)(2,1)} %collective-permute-done.1), channel_id=1, source_target_pairs={{0,64},{64,0},{16,80},{80,16},{32,96},{96,32},{48,112},{112,48},{1... | collective-permute-start | bytes 9400328 | tf_op jit(solution)/shard_map/ppermute | solution.py:14
  328.4 114.4 %collective-permute-start.3 = (bf16[1088,1440]{0,1:T(8,128)(2,1)}, bf16[1088,1440]{0,1:T(8,128)(2,1)}, u32[]{:S(2)}, u32[]{:S(2)}) collective-permute-start(bf16[1088,1440]{0,1:T(8,128)(2,1)} %collective-permute-done.2), channel_id=1, source_target_pairs={{0,128},{128,0},{16,144},{144,16},{32,160},{160,32},{48,176},{176,... | collective-permute-start | bytes 9400328 | tf_op jit(solution)/shard_map/ppermute | solution.py:14
  345.8 8.3 %copy-start.4 = (bf16[1,1088,90]{1,2,0:T(8,128)(2,1)S(1)}, bf16[1,1088,90]{1,2,0:T(8,128)(2,1)}, u32[]{:S(2)}) copy-start(bf16[1,1088,90]{1,2,0:T(8,128)(2,1)} %param.22) | copy-start | bytes 587524
  345.8 117.9 %all-to-all-start.1 = ((bf16[16,68,1440]{2,1,0:T(8,128)(2,1)}), bf16[16,68,1440]{2,1,0:T(8,128)(2,1)}, u32[]{:S(2)}, u32[]{:S(2)}) async-start(bf16[16,68,1440]{2,1,0:T(8,128)(2,1)} %reshape.171), calls=%async_computation.1 | async-start | bytes 7077888 | tf_op jit(solution)/shard_map/all_to_all | solution.py:140
  354.1 1.6 collective-permute-start.4
  355.7 66.6 %collective-permute-start.5 = (bf16[1088,90]{0,1:T(8,128)(2,1)S(1)}, bf16[1088,90]{0,1:T(8,128)(2,1)S(1)}, u32[]{:S(2)}, u32[]{:S(2)}) collective-permute-start(bf16[1088,90]{0,1:T(8,128)(2,1)S(1)} %collective-permute-done.4), channel_id=1, source_target_pairs={{0,32},{32,0},{16,48},{48,16},{64,96},{96,64},{80,112},{112,80},{1... | collective-permute-start | bytes 587528 | tf_op jit(solution)/shard_map/ppermute | solution.py:14
  422.2 8.1 %collective-permute-start.6 = (bf16[1088,90]{0,1:T(8,128)(2,1)S(1)}, bf16[1088,90]{0,1:T(8,128)(2,1)S(1)}, u32[]{:S(2)}, u32[]{:S(2)}) collective-permute-start(bf16[1088,90]{0,1:T(8,128)(2,1)S(1)} %collective-permute-done.5), channel_id=1, source_target_pairs={{0,64},{64,0},{16,80},{80,16},{32,96},{96,32},{48,112},{112,48},{1... | collective-permute-start | bytes 587528 | tf_op jit(solution)/shard_map/ppermute | solution.py:14
  430.3 7.4 %collective-permute-start.7 = (bf16[1088,90]{0,1:T(8,128)(2,1)S(1)}, bf16[1088,90]{0,1:T(8,128)(2,1)S(1)}, u32[]{:S(2)}, u32[]{:S(2)}) collective-permute-start(bf16[1088,90]{0,1:T(8,128)(2,1)S(1)} %collective-permute-done.6), channel_id=1, source_target_pairs={{0,128},{128,0},{16,144},{144,16},{32,160},{160,32},{48,176},{176,... | collective-permute-start | bytes 587528 | tf_op jit(solution)/shard_map/ppermute | solution.py:14
  442.7 2.9 copy-start.2
  442.7 6.7 %slice-start = ((s8[4423680]{0:T(1024)(128)(4,1)}), s8[4194304]{0:T(1024)(128)(4,1)S(1)}, s32[]{:S(2)}) async-start(s8[4423680]{0:T(1024)(128)(4,1)} %bitcast.60), calls=%async_computation.4 | async-start | bytes 8388608
  445.7 3.7 slice-start.1
  463.6 8.3 %copy-start.7 = (f32[1,128,4]{1,2,0:T(4,128)S(1)}, f32[1,128,4]{1,2,0:T(4,128)}, u32[]{:S(2)}) copy-start(f32[1,128,4]{1,2,0:T(4,128)} %param.15) | copy-start | bytes 6148
  463.6 79.8 %all-to-all-start.3 = ((bf16[16,68,1440]{2,1,0:T(8,128)(2,1)}), bf16[16,68,1440]{2,1,0:T(8,128)(2,1)}, u32[]{:S(2)}, u32[]{:S(2)}) async-start(bf16[16,68,1440]{2,1,0:T(8,128)(2,1)} %reshape.178), calls=%async_computation.3 | async-start | bytes 7077888 | tf_op jit(solution)/shard_map/all_to_all | solution.py:159
  557.0 9.7 %copy-start.1 = (bf16[1,1,720,1440]{3,2,1,0:T(8,128)(2,1)S(1)}, bf16[1,1,720,1440]{3,2,1,0:T(8,128)(2,1)}, u32[]{:S(2)}) copy-start(bf16[1,1,720,1440]{3,2,1,0:T(8,128)(2,1)} %param.20) | copy-start | bytes 6220804
where the time goes:
time: 576 us; the launch traced here: 567 us
  waiting for transfers between devices  399 us (69%)
  local copies, waits for them, and re-layouts  70 us (12%)
  starting transfers between devices  45.6 us (8%)
  matrix products  30.6 us (5%)
  other arithmetic  20 us (3%)
    all_to_all x1, waiting for transfers between devices, local(): lax.all_to_all(jnp.repeat(send_now.reshape(experts, capacity, feature_cou...  206 us
    ppermute x8, waiting for transfers between devices, from_partner(): return lax.ppermute(block, axis, route)  140 us
    all_to_all x1, waiting for transfers between devices, local(): lax.all_to_all(input_rows.reshape(devices, capacity, feature_count), 'exp...  52.4 us
    ppermute x8, starting transfers between devices, from_partner(): return lax.ppermute(block, axis, route)  14.4 us
  transfers between devices with their start and end apart: 12, of which 8 were waited for; matrix products, arithmetic and copies ran while one was open for 15% of the time, Pallas kernels for 0%

commit v1 on v0

v1 whole, which is shorter than its diff:
```python
import functools
import jax
import jax.numpy as jnp
from jax import lax
from jax.sharding import PartitionSpec as P
from jax.experimental import pallas as pl
from jax.experimental.pallas import tpu as pltpu

MESH = pl.DeviceIdType.MESH
LINE = 4
BF16 = jnp.bfloat16
F32 = jnp.float32


def dot(a, b, dims=((1,), (0,))):
    return lax.dot_general(a, b, (dims, ((), ())), preferred_element_type=F32)


def kernel(
    sizes,
    table_ref,
    tok_ref,
    grad_ref,
    win_ref,
    wdown_ref,
    codes_ref,
    scales_ref,
    exp_ref,
    moe_ref,
    gin_ref,
    tabs,
    gathered,
    target,
    weight,
    target_t,
    weight_t,
    coef_out,
    coef_in,
    rows_out,
    rows_in,
    back_in,
    total,
    part_out,
    part_up,
    part_down,
    tab_send,
    tab_recv,
    tok_send,
    tok_recv,
    coef_send,
    coef_recv,
    rows_send,
    rows_recv,
    back_send,
    back_recv,
    part_send,
    up_recv,
    down_recv,
):
    pipes, planes, cap, chunk, tok, units, wide, block = sizes
    p = lax.axis_index("pipe")
    e = lax.axis_index("expert")
    y = e // LINE
    z = e % LINE

    def on_z(q):
        return (p, y * LINE + q)

    def on_y(q):
        return (p, q * LINE + z)

    mirror = (pipes - 1 - p, e)

    tabs[z] = table_ref[...]
    gathered[0, z] = tok_ref[...]
    gathered[1, z] = grad_ref[...]

    bar = pltpu.get_barrier_semaphore()
    pl.semaphore_signal(bar, inc=1, device_id=mirror, device_id_type=MESH)
    for i in range(1, planes):
        pl.semaphore_signal(bar, inc=1, device_id=on_y((y + i) % planes), device_id_type=MESH)

    @pl.when(z > 0)
    def _():
        pl.semaphore_signal(bar, inc=1, device_id=on_z(z - 1), device_id_type=MESH)

    @pl.when(z < LINE - 1)
    def _():
        pl.semaphore_signal(bar, inc=1, device_id=on_z(z + 1), device_id_type=MESH)

    @pl.when((z > 0) & (z < LINE - 1))
    def _():
        pl.semaphore_wait(bar, planes + 2)

    @pl.when((z == 0) | (z == LINE - 1))
    def _():
        pl.semaphore_wait(bar, planes + 1)

    def hop_copy(kind, up, zs):
        to = on_z(z + 1) if up else on_z(z - 1)
        way = 0 if up else 1
        if kind == 2:
            return pltpu.make_async_remote_copy(
                tabs.at[zs], tabs.at[zs], tab_send.at[way, zs], tab_recv.at[zs],
                device_id=to, device_id_type=MESH,
            )
        return pltpu.make_async_remote_copy(
            gathered.at[kind, zs], gathered.at[kind, zs], tok_send.at[kind, way, zs],
            tok_recv.at[kind, zs], device_id=to, device_id_type=MESH,
        )

    def hop(kind, d):
        if d == 0:
            @pl.when(z < LINE - 1)
            def _():
                hop_copy(kind, True, z).start()

            @pl.when(z > 0)
            def _():
                hop_copy(kind, False, z).start()
            return

        @pl.when(z >= d)
        def _():
            hop_copy(kind, True, z - d).wait_recv()

            @pl.when(z < LINE - 1)
            def _():
                hop_copy(kind, True, z - d).start()

        @pl.when(z + d <= LINE - 1)
        def _():
            hop_copy(kind, False, z + d).wait_recv()

            @pl.when(z > 0)
            def _():
                hop_copy(kind, False, z + d).start()

    def hop_done(kind):
        for d in range(LINE - 1):
            @pl.when((z < LINE - 1) & (z >= d))
            def _():
                hop_copy(kind, True, z - d).wait_send()

            @pl.when((z > 0) & (z + d <= LINE - 1))
            def _():
                hop_copy(kind, False, z + d).wait_send()

    for kind in (2, 0, 1):
        hop(kind, 0)

    def coef_copy(q):
        return pltpu.make_async_remote_copy(
            coef_out.at[q], coef_in.at[q], coef_send.at[q], coef_recv.at[q],
            device_id=mirror, device_id_type=MESH,
        )

    blocks = scales_ref.shape[1]
    low = lax.broadcasted_iota(jnp.int32, (blocks, 2 * units), 0) * block
    lane = lax.broadcasted_iota(jnp.int32, (blocks, 2 * units), 1)
    spread = jnp.where((lane >= low) & (lane < low + block), 1.0, 0.0).astype(BF16)
    level = exp_ref[...]
    factor = jnp.zeros(level.shape, F32)
    for n in range(-2, 2):
        factor = factor + jnp.where(level == n, F32(2.0**n), F32(0.0))

    def coef_step(i, carry):
        q = (y + 2 * planes - 1 - i) % planes
        r0 = pl.multiple_of(q * chunk, 16)
        scale = dot(scales_ref[pl.ds(r0, chunk), :], spread) * factor
        value = codes_ref[pl.ds(r0, chunk), :].astype(F32) * scale
        gate = value[:, :units]
        up = value[:, units:]
        sig = 1.0 / (1.0 + jnp.exp(-gate))
        coef_out[q, :, 0:units] = (up * sig * (1.0 + gate * (1.0 - sig))).astype(BF16)
        coef_out[q, :, wide : wide + units] = (gate * sig).astype(BF16)

        @pl.when((z == 0) | (z == LINE - 1))
        def _():
            coef_copy(q).start()
        return carry

    lax.fori_loop(0, planes, coef_step, 0)

    for d in (1, 2):
        for kind in (2, 0, 1):
            hop(kind, d)

    @pl.when((z > 0) & (z < LINE - 1))
    def _():
        for i in range(planes):
            coef_copy((y + 2 * planes - 1 - i) % planes).start()

    hop(2, 3)

    plane_expert = (
        2 * lax.broadcasted_iota(jnp.int32, (8, tok), 0) + z // 2
    ).astype(F32)
    earlier = jnp.where(
        lax.broadcasted_iota(jnp.int32, (tok, tok), 0)
        < lax.broadcasted_iota(jnp.int32, (tok, tok), 1),
        1.0,
        0.0,
    ).astype(BF16)
    for ph in range(2):
        for zs in range(LINE):
            member = jnp.zeros((8, tok), F32)
            prob = jnp.zeros((8, tok), F32)
            for k in range(4):
                hit = tabs[zs, 8 * ph + k : 8 * ph + k + 1, :] == plane_expert
                member = member + jnp.where(hit, 1.0, 0.0)
                prob = prob + jnp.where(hit, tabs[zs, 8 * ph + 4 + k : 8 * ph + 5 + k, :], 0.0)
            before = dot(member.astype(BF16), earlier)
            target[ph, :, zs * tok : (zs + 1) * tok] = jnp.where(
                member > 0.5, before + F32(zs * cap), F32(-1.0)
            )
            weight[ph, :, zs * tok : (zs + 1) * tok] = prob
        target_t[ph] = target[ph].T
        weight_t[ph] = weight[ph].T

    def rows_copy(ph, q):
        return pltpu.make_async_remote_copy(
            rows_out.at[ph, q], rows_in.at[ph, y], rows_send.at[ph, q], rows_recv.at[ph, y],
            device_id=on_y(q), device_id_type=MESH,
        )

    def rows_arrived(ph, q):
        return pltpu.make_async_remote_copy(
            rows_out.at[ph, q], rows_in.at[ph, q], rows_send.at[ph, q], rows_recv.at[ph, q],
            device_id=on_y(q), device_id_type=MESH,
        )

    def back_copy(ph, q):
        return pltpu.make_async_remote_copy(
            rows_in.at[ph, q], back_in.at[ph, y], back_send.at[ph, q], back_recv.at[ph, y],
            device_id=on_y(q), device_id_type=MESH,
        )

    def back_arrived(ph, q):
        return pltpu.make_async_remote_copy(
            rows_in.at[ph, q], back_in.at[ph, q], back_send.at[ph, q], back_recv.at[ph, q],
            device_id=on_y(q), device_id_type=MESH,
        )

    line_tok = LINE * tok
    slot_row = lax.broadcasted_iota(jnp.int32, (chunk, line_tok), 0).astype(F32)

    def send_rows(ph):
        def step(i, carry):
            q = (y + 1 + i) % planes
            match = slot_row == target[ph, pl.ds(q, 1), :]
            rows = dot(
                jnp.where(match, 1.0, 0.0).astype(BF16),
                gathered[ph].reshape(line_tok, gathered.shape[-1]),
            )
            if ph == 1:
                rows = rows * jnp.sum(
                    jnp.where(match, weight[ph, pl.ds(q, 1), :], 0.0), axis=1, keepdims=True
                )
            rows_out[ph, q] = rows.astype(BF16)

            @pl.when(i < planes - 1)
            def _():
                rows_copy(ph, q).start()
            return carry

        lax.fori_loop(0, planes, step, 0)
        rows_in[ph, y] = rows_out[ph, y]

    hop(0, 3)
    send_rows(0)
    hop(1, 3)
    send_rows(1)

    def forward_step(i, carry):
        q = (y + planes - i) % planes

        @pl.when(i > 0)
        def _():
            rows_arrived(0, q).wait_recv()

        both = dot(rows_in[0, q], win_ref[...])
        gate = both[:, :units]
        hidden = (gate * (1.0 / (1.0 + jnp.exp(-gate))) * both[:, units:]).astype(BF16)
        rows_in[0, q] = dot(hidden, wdown_ref[...]).astype(BF16)

        @pl.when(i > 0)
        def _():
            back_copy(0, q).start()
        return carry

    lax.fori_loop(0, planes, forward_step, 0)

    lane_row = lax.broadcasted_iota(jnp.int32, (line_tok, chunk), 1).astype(F32)
    column = lax.broadcasted_iota(jnp.int32, (line_tok, 8), 1)

    def combine(ph):
        back_in[ph, y] = rows_in[ph, y]
        total[ph] = jnp.zeros(total.shape[1:], F32)

        def step(i, carry):
            q = (y + i) % planes

            @pl.when(i > 0)
            def _():
                back_arrived(ph, q).wait_recv()

            place = jnp.sum(jnp.where(column == q, target_t[ph], 0.0), axis=1, keepdims=True)
            match = lane_row == place
            rows = back_in[ph, q]
            if ph == 0:
                prob = jnp.sum(jnp.where(column == q, weight_t[ph], 0.0), axis=1, keepdims=True)
                full = jnp.where(match, prob, 0.0)
                high = full.astype(BF16)
                rest = (full - high.astype(F32)).astype(BF16)
                value = dot(high, rows) + dot(rest, rows)
            else:
                value = dot(jnp.where(match, 1.0, 0.0).astype(BF16), rows)
            total[ph] += value.reshape(total.shape[1:])
            return carry

        lax.fori_loop(0, planes, step, 0)

    def part_copy(ph, up, d):
        if up:
            return pltpu.make_async_remote_copy(
                part_out.at[ph, d], part_up.at[ph, d], part_send.at[ph, d], up_recv.at[ph, d],
                device_id=on_z(z + 1), device_id_type=MESH,
            )
        return pltpu.make_async_remote_copy(
            part_out.at[ph, d], part_down.at[ph, d], part_send.at[ph, d], down_recv.at[ph, d],
            device_id=on_z(z - 1), device_id_type=MESH,
        )

    def send_up(ph, d):
        @pl.when(z == 0)
        def _():
            part_out[ph, d] = total[ph, d].astype(BF16)

        @pl.when((z > 0) & (z < d))
        def _():
            part_copy(ph, True, d).wait_recv()
            part_out[ph, d] = (total[ph, d] + part_up[ph, d].astype(F32)).astype(BF16)

        @pl.when(z < d)
        def _():
            part_copy(ph, True, d).start()

    def send_down(ph, d):
        @pl.when(z == LINE - 1)
        def _():
            part_out[ph, d] = total[ph, d].astype(BF16)

        @pl.when((z < LINE - 1) & (z > d))
        def _():
            part_copy(ph, False, d).wait_recv()
            part_out[ph, d] = (total[ph, d] + part_down[ph, d].astype(F32)).astype(BF16)

        @pl.when(z > d)
        def _():
            part_copy(ph, False, d).start()

    def reduce_line(ph):
        for s in range(LINE - 1):
            @pl.when((z > 0) & (z < LINE // 2))
            def _():
                send_up(ph, LINE - 1 - s)
                send_down(ph, s)

            @pl.when((z >= LINE // 2) & (z < LINE - 1))
            def _():
                send_down(ph, s)
                send_up(ph, LINE - 1 - s)

    def reduce_ends(ph):
        @pl.when(z == 0)
        def _():
            for s in range(LINE - 1):
                send_up(ph, LINE - 1 - s)

        @pl.when(z == LINE - 1)
        def _():
            for s in range(LINE - 1):
                send_down(ph, s)

    def finish_line(ph, out_ref):
        @pl.when(z > 0)
        def _():
            part_copy(ph, True, z).wait_recv()
            total[ph, z] += part_up[ph, z].astype(F32)

        @pl.when(z < LINE - 1)
        def _():
            part_copy(ph, False, z).wait_recv()
            total[ph, z] += part_down[ph, z].astype(F32)

        out_ref[...] = total[ph, z].astype(BF16)

    combine(0)

    reduce_ends(0)

    def backward_step(i, carry):
        q = (y + 2 * planes - 1 - i) % planes

        @pl.when(i < planes - 1)
        def _():
            rows_arrived(1, q).wait_recv()

        hidden = dot(rows_in[1, q], wdown_ref[...], ((1,), (1,)))
        coef_copy(q).wait_recv()
        joined = jnp.concatenate(
            [
                hidden * coef_in[q, :, 0:units].astype(F32),
                hidden * coef_in[q, :, wide : wide + units].astype(F32),
            ],
            axis=1,
        ).astype(BF16)
        rows_in[1, q] = dot(joined, win_ref[...], ((1,), (1,))).astype(BF16)

        @pl.when(i < planes - 1)
        def _():
            back_copy(1, q).start()
        return carry

    lax.fori_loop(0, planes, backward_step, 0)
    combine(1)
    reduce_ends(1)
    reduce_line(0)
    reduce_line(1)
    finish_line(0, moe_ref)
    finish_line(1, gin_ref)

    for kind in range(3):
        hop_done(kind)
    for q in range(planes):
        coef_copy(q).wait_send()
    for ph in range(2):
        for i in range(1, planes):
            rows_copy(ph, (y + i) % planes).wait_send()
            back_copy(ph, (y + i) % planes).wait_send()
        for d in range(LINE):
            @pl.when(z < d)
            def _():
                part_copy(ph, True, d).wait_send()

            @pl.when(z > d)
            def _():
                part_copy(ph, False, d).wait_send()


def local(
    tokens,
    routes_fwd,
    probs_fwd,
    grad_out,
    routes_bwd,
    probs_bwd,
    w_in,
    w_down,
    saved_codes,
    saved_scales,
    saved_exponent,
):
    devices = lax.axis_size("expert")
    planes = devices // LINE
    tok, depth = tokens.shape[1:]
    units = w_down.shape[2]
    rows = saved_codes.shape[1]
    cap = rows // devices
    chunk = cap * LINE
    wide = -(-units // 128) * 128
    block = 2 * units // saved_scales.shape[2]
    table = jnp.concatenate(
        [
            routes_fwd[0].astype(F32),
            probs_fwd[0],
            routes_bwd[0].astype(F32),
            probs_bwd[0],
        ],
        axis=1,
    ).T
    sizes = (lax.axis_size("pipe"), planes, cap, chunk, tok, units, wide, block)
    vmem = pl.BlockSpec(memory_space=pltpu.VMEM)
    dma = pltpu.SemaphoreType.DMA
    moe, gin = pl.pallas_call(
        functools.partial(kernel, sizes),
        out_shape=[jax.ShapeDtypeStruct((tok, depth), BF16)] * 2,
        in_specs=[vmem] * 8,
        out_specs=[vmem] * 2,
        scratch_shapes=[
            pltpu.VMEM((LINE, 16, tok), F32),
            pltpu.VMEM((2, LINE, tok, depth), BF16),
            pltpu.VMEM((2, 8, LINE * tok), F32),
            pltpu.VMEM((2, 8, LINE * tok), F32),
            pltpu.VMEM((2, LINE * tok, 8), F32),
            pltpu.VMEM((2, LINE * tok, 8), F32),
            pltpu.VMEM((planes, chunk, 2 * wide), BF16),
            pltpu.VMEM((planes, chunk, 2 * wide), BF16),
            pltpu.VMEM((2, planes, chunk, depth), BF16),
            pltpu.VMEM((2, planes, chunk, depth), BF16),
            pltpu.VMEM((2, planes, chunk, depth), BF16),
            pltpu.VMEM((2, LINE, tok, depth), F32),
            pltpu.VMEM((2, LINE, tok, depth), BF16),
            pltpu.VMEM((2, LINE, tok, depth), BF16),
            pltpu.VMEM((2, LINE, tok, depth), BF16),
            dma((2, LINE)),
            dma((LINE,)),
            dma((2, 2, LINE)),
            dma((2, LINE)),
            dma((planes,)),
            dma((planes,)),
            dma((2, planes)),
            dma((2, planes)),
            dma((2, planes)),
            dma((2, planes)),
            dma((2, LINE)),
            dma((2, LINE)),
            dma((2, LINE)),
        ],
        compiler_params=pltpu.CompilerParams(
            collective_id=0, has_side_effects=True, vmem_limit_bytes=62 << 20
        ),
        cost_estimate=pl.CostEstimate(
            flops=8 * rows * units * depth * 3, bytes_accessed=16 << 20, transcendentals=0
        ),
    )(
        table,
        tokens[0],
        grad_out[0],
        w_in[0, 0],
        w_down[0, 0],
        saved_codes[0],
        saved_scales[0],
        saved_exponent,
    )
    return (moe[None], gin[None])


def solution(mesh):
    rows3 = P("pipe", "expert", None)
    rows4 = P("pipe", "expert", None, None)
    in_specs = (rows3,) * 6 + (rows4, rows4, rows3, rows3, P("pipe", "expert"))
    return jax.shard_map(
        local, mesh=mesh, in_specs=in_specs, out_specs=(rows3, rows3), check_vma=False
    )
```

time: 576 us -> 336 us (0.58)
  waiting for transfers between devices: 399 us -> 0 us
  Pallas kernels: 0 us -> 314 us
  local copies, waits for them, and re-layouts: 70 us -> 15.1 us
  starting transfers between devices: 45.6 us -> 0 us
  matrix products: 30.6 us -> 0 us
  other arithmetic: 20 us -> 2.01 us
    pallas_call x0 -> x1, Pallas kernels: none -> 314 us  [local(): pl.pallas_call(functools.partial(kernel, sizes), out_shape=[jax.ShapeDtyp...]
    all_to_all x4 -> x0, waiting for transfers between devices: 259 us -> none  [the longest x1 206 us: local(): lax.all_to_all(jnp.repeat(send_now.reshape(experts, capacity, feature_cou...]
    ppermute x8 -> x0, waiting for transfers between devices: 140 us -> none  [from_partner(): return lax.ppermute(block, axis, route)]
    reshape x10 -> x0, local copies, waits for them, and re-layouts: 36.2 us -> none  [the longest x2 6.89 us: gather_pairs(): table_rows = returned.reshape(-1, returned.shape[-1])]
    all_to_all x4 -> x0, starting transfers between devices: 31.2 us -> none  [the longest x1 8.9 us: local(): lax.all_to_all(jnp.repeat(send_now.reshape(experts, capacity, feature_cou...]
    dot_general x6 -> x0, matrix products: 30.6 us -> none  [the longest x1 9.93 us: expert_forward(): gate_up = jnp.dot(inputs, weight_in, preferred_element_type=jnp.float32)]
    ppermute x8 -> x0, starting transfers between devices: 14.4 us -> none  [from_partner(): return lax.ppermute(block, axis, route)]
    gather x4 -> x0, local copies, waits for them, and re-layouts: 11.8 us -> none  [the longest x2 5.95 us: gather_pairs(): first_half = jnp.take(table_rows, even_rows, axis=0).astype(jnp.float32)]
  transfers between devices with their start and end apart: 12 -> 0, of which waited for: 8 -> 0; matrix products, arithmetic and copies ran while one was open for 15% -> 0% of each run, Pallas kernels for 0% -> 0%
where the time goes in v1:
time: 336 us; the launch traced here: 332 us
  Pallas kernels  314 us (93%)
  local copies, waits for them, and re-layouts  15.1 us (4%)
    pallas_call x1, Pallas kernels, local(): pl.pallas_call(functools.partial(kernel, sizes), out_shape=[jax.ShapeDtyp...  314 us
    unnamed x6, local copies, waits for them, and re-layouts  15.1 us

profile of v1, /device:TPU:26, one launch (start us, length us, event | category | flops | bytes accessed | tf_op | source)
XLA Modules:
  0.0 332.2 jit_solution(14838945311577486412)
XLA Ops:
  1.3 0.7 convert_bitcast_fusion
  2.0 1.3 maximum_bitcast_fusion.table_ref
  3.3 1.8 copy.16
  5.1 1.9 copy.13
  7.0 1.9 copy.14
  8.9 5.6 %copy.15 = bf16[1,1088,1440]{2,1,0:T(8,128)(2,1)} copy(bf16[1,1088,1440]{1,2,0:T(8,128)(2,1)} %param.19) | data formatting | bytes 6266880 | tf_op args[8]
  14.6 313.8 %shard_map.122 = (bf16[128,1440]{1,0:T(8,128)(2,1)}, bf16[128,1440]{1,0:T(8,128)(2,1)}) custom-call(f32[16,128]{1,0:T(8,128)} %maximum_bitcast_fusion.table_ref, bf16[128,1440]{1,0:T(8,128)(2,1)} %bitcast.19, bf16[128,1440]{1,0:T(8,128)(2,1)} %bitcast.20, bf16[1440,1440]{1,0:T(8,128)(2,1)} %bitcast.24, bf16[720,1440]{1,0:T(8,128)(2,1)} %bitcast.25, ...), custom_call_target="tpu_custom_call" | custom-call | flops 27072921600 | bytes 16777216 | tf_op jit(solution)/shard_map/pallas_call | solution.py:486
  328.4 1.9 copy.17
  330.3 1.9 copy.18

commit v2 on v1

--- a/solution.py
+++ b/solution.py
@@ -18,16 +18,25 @@
 
 def kernel(
     sizes,
-    table_ref,
+    route_now_ref,
+    prob_now_ref,
+    route_old_ref,
+    prob_old_ref,
     tok_ref,
     grad_ref,
-    win_ref,
-    wdown_ref,
-    codes_ref,
+    win_hbm,
+    wdown_hbm,
+    codes_hbm,
     scales_ref,
     exp_ref,
     moe_ref,
     gin_ref,
+    win_ref,
+    wdown_ref,
+    codes_ref,
+    final,
+    rest_all,
+    load_sem,
     tabs,
     gathered,
     target,
@@ -36,6 +45,8 @@
     weight_t,
     coef_out,
     coef_in,
+    rest_out,
+    rest_in,
     rows_out,
     rows_in,
     back_in,
@@ -49,6 +60,8 @@
     tok_recv,
     coef_send,
     coef_recv,
+    rest_send,
+    rest_recv,
     rows_send,
     rows_recv,
     back_send,
@@ -57,7 +70,10 @@
     up_recv,
     down_recv,
 ):
-    pipes, planes, cap, chunk, tok, units, wide, block = sizes
+    pipes, planes, cap, chunk, tok, units, block = sizes
+    main = units // 128 * 128
+    body = 2 * units // 128 * 128
+    rest = 2 * units - body
     p = lax.axis_index("pipe")
     e = lax.axis_index("expert")
     y = e // LINE
@@ -71,7 +87,17 @@
 
     mirror = (pipes - 1 - p, e)
 
-    tabs[z] = table_ref[...]
+    loads = [
+        pltpu.make_async_copy(src, dst, load_sem.at[n])
+        for n, (src, dst) in enumerate(
+            ((codes_hbm, codes_ref), (win_hbm, win_ref), (wdown_hbm, wdown_ref))
+        )
+    ]
+    for load in loads:
+        load.start()
+
+    for n, part in enumerate((route_now_ref, prob_now_ref, route_old_ref, prob_old_ref)):
+        tabs[z, 4 * n : 4 * n + 4, :] = part[...].astype(F32)
     gathered[0, z] = tok_ref[...]
     gathered[1, z] = grad_ref[...]
 
@@ -146,51 +172,74 @@
             def _():
                 hop_copy(kind, False, z + d).wait_send()
 
-    for kind in (2, 0, 1):
-        hop(kind, 0)
+    inner = (z > 0) & (z < LINE - 1)
+    ends = (z == 0) | (z == LINE - 1)
+    hop(2, 0)
+    hop(0, 0)
+
+    @pl.when(ends)
+    def _():
+        hop(1, 0)
 
     def coef_copy(q):
         return pltpu.make_async_remote_copy(
-            coef_out.at[q], coef_in.at[q], coef_send.at[q], coef_recv.at[q],
+            coef_out.at[pl.ds(pl.multiple_of(q * chunk, 16), chunk)], coef_in.at[q], coef_send.at[q], coef_recv.at[q],
             device_id=mirror, device_id_type=MESH,
         )
 
-    blocks = scales_ref.shape[1]
-    low = lax.broadcasted_iota(jnp.int32, (blocks, 2 * units), 0) * block
-    lane = lax.broadcasted_iota(jnp.int32, (blocks, 2 * units), 1)
-    spread = jnp.where((lane >= low) & (lane < low + block), 1.0, 0.0).astype(BF16)
+    blocks = scales_ref.shape[0]
+    low = lax.broadcasted_iota(jnp.int32, (2 * units, blocks), 1) * block
+    line = lax.broadcasted_iota(jnp.int32, (2 * units, blocks), 0)
+    spread = jnp.where((line >= low) & (line < low + block), 1.0, 0.0).astype(BF16)
     level = exp_ref[...]
     factor = jnp.zeros(level.shape, F32)
     for n in range(-2, 2):
         factor = factor + jnp.where(level == n, F32(2.0**n), F32(0.0))
 
-    def coef_step(i, carry):
-        q = (y + 2 * planes - 1 - i) % planes
-        r0 = pl.multiple_of(q * chunk, 16)
-        scale = dot(scales_ref[pl.ds(r0, chunk), :], spread) * factor
-        value = codes_ref[pl.ds(r0, chunk), :].astype(F32) * scale
-        gate = value[:, :units]
-        up = value[:, units:]
+    def coef_tile(start, size):
+        here = pl.ds(start, size)
+        value = codes_ref[:, here].astype(F32) * (dot(spread, scales_ref[:, here]) * factor)
+        gate = value[:units]
+        up = value[units:]
         sig = 1.0 / (1.0 + jnp.exp(-gate))
-        coef_out[q, :, 0:units] = (up * sig * (1.0 + gate * (1.0 - sig))).astype(BF16)
-        coef_out[q, :, wide : wide + units] = (gate * sig).astype(BF16)
-
-        @pl.when((z == 0) | (z == LINE - 1))
-        def _():
-            coef_copy(q).start()
+        one = (up * sig * (1.0 + gate * (1.0 - sig))).T
+        two = (gate * sig).T
+        coef_out[here, 0:main] = one[:, :main].astype(BF16)
+        coef_out[here, main : 2 * main] = two[:, :main].astype(BF16)
+        ending = jnp.concatenate([one[:, main:], two[:, main:]], axis=1)
+        coef_out[here, 2 * main : body] = ending[:, : body - 2 * main].astype(BF16)
+        rest_all[here, :] = ending[:, body - 2 * main :].astype(BF16)
+
+    def coef_step(t, carry):
+        coef_tile(pl.multiple_of(t * 128, 128), 128)
         return carry
 
-    lax.fori_loop(0, planes, coef_step, 0)
-
-    for d in (1, 2):
-        for kind in (2, 0, 1):
-            hop(kind, d)
-
-    @pl.when((z > 0) & (z < LINE - 1))
-    def _():
-        for i in range(planes):
-            coef_copy((y + 2 * planes - 1 - i) % planes).start()
-
+    def coef_start(i):
+        coef_copy((y + 2 * planes - 1 - i) % planes).start()
+
+    rest_copy = pltpu.make_async_remote_copy(
+        rest_out, rest_in, rest_send, rest_recv, device_id=mirror, device_id_type=MESH
+    )
+    loads[0].wait()
+    rows = codes_ref.shape[1]
+    half = rows // 256
+    lax.fori_loop(0, half, coef_step, 0)
+    hop(2, 1)
+    hop(0, 1)
+
+    @pl.when(inner)
+    def _():
+        hop(1, 0)
+
+    lax.fori_loop(half, rows // 128, coef_step, 0)
+    if rows % 128:
+        coef_tile(rows // 128 * 128, rows % 128)
+    rest_out[...] = jnp.concatenate(
+        [rest_all[q * chunk : (q + 1) * chunk, :] for q in range(planes)], axis=1
+    )
+
+    hop(2, 2)
+    hop(0, 2)
     hop(2, 3)
 
     plane_expert = (
@@ -251,7 +300,8 @@
             match = slot_row == target[ph, pl.ds(q, 1), :]
             rows = dot(
                 jnp.where(match, 1.0, 0.0).astype(BF16),
-                gathered[ph].reshape(line_tok, gathered.shape[-1]),
+                jnp.concatenate([gathered[ph, zs] for zs in range(LINE)], axis=1),
+                ((1,), (1,)),
             )
             if ph == 1:
                 rows = rows * jnp.sum(
@@ -269,8 +319,26 @@
 
     hop(0, 3)
     send_rows(0)
+
+    @pl.when(ends)
+    def _():
+        rest_copy.start()
+        coef_start(0)
+        coef_start(1)
+
+    hop(1, 1)
+    hop(1, 2)
+
+    @pl.when(inner)
+    def _():
+        rest_copy.start()
+        coef_start(0)
+        coef_start(1)
+
     hop(1, 3)
     send_rows(1)
+    loads[1].wait()
+    loads[2].wait()
 
     def forward_step(i, carry):
         q = (y + planes - i) % planes
@@ -290,18 +358,17 @@
         return carry
 
     lax.fori_loop(0, planes, forward_step, 0)
+    coef_start(2)
+    coef_start(3)
 
     lane_row = lax.broadcasted_iota(jnp.int32, (line_tok, chunk), 1).astype(F32)
     column = lax.broadcasted_iota(jnp.int32, (line_tok, 8), 1)
 
-    def combine(ph):
-        back_in[ph, y] = rows_in[ph, y]
-        total[ph] = jnp.zeros(total.shape[1:], F32)
-
+    def combine(ph, first, last):
         def step(i, carry):
             q = (y + i) % planes
 
-            @pl.when(i > 0)
+            @pl.when(i % planes > 0)
             def _():
                 back_arrived(ph, q).wait_recv()
 
@@ -319,7 +386,7 @@
             total[ph] += value.reshape(total.shape[1:])
             return carry
 
-        lax.fori_loop(0, planes, step, 0)
+        lax.fori_loop(first, last, step, 0)
 
     def part_copy(ph, up, d):
         if up:
@@ -335,12 +402,12 @@
     def send_up(ph, d):
         @pl.when(z == 0)
         def _():
-            part_out[ph, d] = total[ph, d].astype(BF16)
+            part_out[ph, d] = total[ph, d].T.astype(BF16)
 
         @pl.when((z > 0) & (z < d))
         def _():
             part_copy(ph, True, d).wait_recv()
-            part_out[ph, d] = (total[ph, d] + part_up[ph, d].astype(F32)).astype(BF16)
+            part_out[ph, d] = (total[ph, d].T + part_up[ph, d].astype(F32)).astype(BF16)
 
         @pl.when(z < d)
         def _():
@@ -349,12 +416,12 @@
     def send_down(ph, d):
         @pl.when(z == LINE - 1)
         def _():
-            part_out[ph, d] = total[ph, d].astype(BF16)
+            part_out[ph, d] = total[ph, d].T.astype(BF16)
 
         @pl.when((z < LINE - 1) & (z > d))
         def _():
             part_copy(ph, False, d).wait_recv()
-            part_out[ph, d] = (total[ph, d] + part_down[ph, d].astype(F32)).astype(BF16)
+            part_out[ph, d] = (total[ph, d].T + part_down[ph, d].astype(F32)).astype(BF16)
 
         @pl.when(z > d)
         def _():
@@ -384,21 +451,28 @@
                 send_down(ph, s)
 
     def finish_line(ph, out_ref):
+        final[...] = total[ph, z].T
+
         @pl.when(z > 0)
         def _():
             part_copy(ph, True, z).wait_recv()
-            total[ph, z] += part_up[ph, z].astype(F32)
+            final[...] += part_up[ph, z].astype(F32)
 
         @pl.when(z < LINE - 1)
         def _():
             part_copy(ph, False, z).wait_recv()
-            total[ph, z] += part_down[ph, z].astype(F32)
-
-        out_ref[...] = total[ph, z].astype(BF16)
-
-    combine(0)
-
-    reduce_ends(0)
+            final[...] += part_down[ph, z].astype(F32)
+
+        out_ref[...] = final[...].astype(BF16)
+
+    def rest_of(q):
+        full = rest_in[...].astype(F32)
+        picked = full[:, :rest]
+        for n in range(1, planes):
+            picked = jnp.where(q == n, full[:, n * rest : (n + 1) * rest], picked)
+        return picked
+
+    rest_copy.wait_recv()
 
     def backward_step(i, carry):
         q = (y + 2 * planes - 1 - i) % planes
@@ -409,10 +483,15 @@
 
         hidden = dot(rows_in[1, q], wdown_ref[...], ((1,), (1,)))
         coef_copy(q).wait_recv()
+        ending = coef_in[q, :, 2 * main : body].astype(F32)
+        tail = units - main
         joined = jnp.concatenate(
             [
-                hidden * coef_in[q, :, 0:units].astype(F32),
-                hidden * coef_in[q, :, wide : wide + units].astype(F32),
+                hidden[:, :main] * coef_in[q, :, 0:main].astype(F32),
+                hidden[:, main:] * ending[:, :tail],
+                hidden[:, :main] * coef_in[q, :, main : 2 * main].astype(F32),
+                hidden[:, main : units - rest] * ending[:, tail:],
+                hidden[:, units - rest :] * rest_of(q),
             ],
             axis=1,
         ).astype(BF16)
@@ -423,8 +502,16 @@
             back_copy(1, q).start()
         return carry
 
-    lax.fori_loop(0, planes, backward_step, 0)
-    combine(1)
+    lax.fori_loop(0, 2, backward_step, 0)
+    back_in[0, y] = rows_in[0, y]
+    total[...] = jnp.zeros_like(total)
+    combine(0, 0, planes)
+    reduce_ends(0)
+    lax.fori_loop(2, 3, backward_step, 0)
+    combine(1, 1, planes)
+    lax.fori_loop(3, planes, backward_step, 0)
+    back_in[1, y] = rows_in[1, y]
+    combine(1, planes, planes + 1)
     reduce_ends(1)
     reduce_line(0)
     reduce_line(1)
@@ -433,6 +520,7 @@
 
     for kind in range(3):
         hop_done(kind)
+    rest_copy.wait_send()
     for q in range(planes):
         coef_copy(q).wait_send()
     for ph in range(2):
@@ -469,47 +557,49 @@
     rows = saved_codes.shape[1]
     cap = rows // devices
     chunk = cap * LINE
-    wide = -(-units // 128) * 128
+    body = 2 * units // 128 * 128
+    rest = 2 * units - body
     block = 2 * units // saved_scales.shape[2]
-    table = jnp.concatenate(
-        [
-            routes_fwd[0].astype(F32),
-            probs_fwd[0],
-            routes_bwd[0].astype(F32),
-            probs_bwd[0],
-        ],
-        axis=1,
-    ).T
-    sizes = (lax.axis_size("pipe"), planes, cap, chunk, tok, units, wide, block)
+    sizes = (lax.axis_size("pipe"), planes, cap, chunk, tok, units, block)
     vmem = pl.BlockSpec(memory_space=pltpu.VMEM)
     dma = pltpu.SemaphoreType.DMA
     moe, gin = pl.pallas_call(
         functools.partial(kernel, sizes),
-        out_shape=[jax.ShapeDtypeStruct((tok, depth), BF16)] * 2,
-        in_specs=[vmem] * 8,
+        out_shape=[jax.ShapeDtypeStruct((depth, tok), BF16)] * 2,
+        in_specs=[vmem] * 6 + [pl.BlockSpec(memory_space=pl.ANY)] * 3 + [vmem] * 2,
         out_specs=[vmem] * 2,
         scratch_shapes=[
+            pltpu.VMEM((depth, 2 * units), BF16),
+            pltpu.VMEM((units, depth), BF16),
+            pltpu.VMEM((2 * units, rows), BF16),
+            pltpu.VMEM((depth, tok), F32),
+            pltpu.VMEM((rows, rest), BF16),
+            dma((3,)),
             pltpu.VMEM((LINE, 16, tok), F32),
-            pltpu.VMEM((2, LINE, tok, depth), BF16),
+            pltpu.VMEM((2, LINE, depth, tok), BF16),
             pltpu.VMEM((2, 8, LINE * tok), F32),
             pltpu.VMEM((2, 8, LINE * tok), F32),
             pltpu.VMEM((2, LINE * tok, 8), F32),
             pltpu.VMEM((2, LINE * tok, 8), F32),
-            pltpu.VMEM((planes, chunk, 2 * wide), BF16),
-            pltpu.VMEM((planes, chunk, 2 * wide), BF16),
+            pltpu.VMEM((rows, body), BF16),
+            pltpu.VMEM((planes, chunk, body), BF16),
+            pltpu.VMEM((chunk, planes * rest), BF16),
+            pltpu.VMEM((chunk, planes * rest), BF16),
             pltpu.VMEM((2, planes, chunk, depth), BF16),
             pltpu.VMEM((2, planes, chunk, depth), BF16),
             pltpu.VMEM((2, planes, chunk, depth), BF16),
             pltpu.VMEM((2, LINE, tok, depth), F32),
-            pltpu.VMEM((2, LINE, tok, depth), BF16),
-            pltpu.VMEM((2, LINE, tok, depth), BF16),
-            pltpu.VMEM((2, LINE, tok, depth), BF16),
+            pltpu.VMEM((2, LINE, depth, tok), BF16),
+            pltpu.VMEM((2, LINE, depth, tok), BF16),
+            pltpu.VMEM((2, LINE, depth, tok), BF16),
             dma((2, LINE)),
             dma((LINE,)),
             dma((2, 2, LINE)),
             dma((2, LINE)),
             dma((planes,)),
             dma((planes,)),
+            dma,
+            dma,
             dma((2, planes)),
             dma((2, planes)),
             dma((2, planes)),
@@ -525,16 +615,19 @@
             flops=8 * rows * units * depth * 3, bytes_accessed=16 << 20, transcendentals=0
         ),
     )(
-        table,
-        tokens[0],
-        grad_out[0],
+        routes_fwd[0].T,
+        probs_fwd[0].T,
+        routes_bwd[0].T,
+        probs_bwd[0].T,
+        tokens[0].T,
+        grad_out[0].T,
         w_in[0, 0],
         w_down[0, 0],
-        saved_codes[0],
-        saved_scales[0],
+        saved_codes[0].T,
+        saved_scales[0].T,
         saved_exponent,
     )
-    return (moe[None], gin[None])
+    return (moe.T[None], gin.T[None])
 
 
 def solution(mesh):

time: 336 us -> 254 us (0.76)
  Pallas kernels: 314 us -> 248 us
  local copies, waits for them, and re-layouts: 15.1 us -> 3.5 us
    pallas_call x1, Pallas kernels: 314 us -> 248 us  [local(): pl.pallas_call(functools.partial(kernel, sizes), out_shape=[jax.ShapeDtyp...]
    unnamed x6 -> x2, local copies, waits for them, and re-layouts: 15.1 us -> 3.5 us
where the time goes in v2:
time: 254 us; the launch traced here: 252 us
  Pallas kernels  248 us (98%)
  local copies, waits for them, and re-layouts  3.5 us (1%)
    pallas_call x1, Pallas kernels, local(): pl.pallas_call(functools.partial(kernel, sizes), out_shape=[jax.ShapeDtyp...  248 us

profile of v2, /device:TPU:26, one launch (start us, length us, event | category | flops | bytes accessed | tf_op | source)
XLA Modules:
  0.0 252.3 jit_solution(2265669879410393976)
XLA Ops:
  1.3 247.5 %shard_map.122 = (bf16[1440,128]{1,0:T(8,128)(2,1)}, bf16[1440,128]{1,0:T(8,128)(2,1)}) custom-call(s32[4,128]{1,0:T(4,128)} %bitcast.40, f32[4,128]{1,0:T(4,128)} %bitcast.41, s32[4,128]{1,0:T(4,128)} %bitcast.42, f32[4,128]{1,0:T(4,128)} %bitcast.43, bf16[1440,128]{1,0:T(8,128)(2,1)} %bitcast.37, bf16[1440,128]{1,0:T(8,128)(2,1)} %bitcast.38, ...), custom_call_target="tpu_custom_call" | custom-call | flops 27072921600 | bytes 16777216 | tf_op jit(solution)/shard_map/pallas_call | solution.py:566
  248.8 1.7 copy.16
  250.6 1.7 copy.17

commit v3 on v2

--- a/solution.py
+++ b/solution.py
@@ -29,8 +29,7 @@
     codes_hbm,
     scales_ref,
     exp_ref,
-    moe_ref,
-    gin_ref,
+    out_ref,
     win_ref,
     wdown_ref,
     codes_ref,
@@ -51,6 +50,7 @@
     rows_in,
     back_in,
     total,
+    turned,
     part_out,
     part_up,
     part_down,
@@ -383,10 +383,14 @@
                 value = dot(high, rows) + dot(rest, rows)
             else:
                 value = dot(jnp.where(match, 1.0, 0.0).astype(BF16), rows)
-            total[ph] += value.reshape(total.shape[1:])
+            total[...] += value.reshape(total.shape)
             return carry
 
         lax.fori_loop(first, last, step, 0)
+
+    def turn(ph):
+        for d in range(LINE):
+            turned[ph, d] = total[d].T
 
     def part_copy(ph, up, d):
         if up:
@@ -402,12 +406,12 @@
     def send_up(ph, d):
         @pl.when(z == 0)
         def _():
-            part_out[ph, d] = total[ph, d].T.astype(BF16)
+            part_out[ph, d] = total[d].T.astype(BF16)
 
         @pl.when((z > 0) & (z < d))
         def _():
             part_copy(ph, True, d).wait_recv()
-            part_out[ph, d] = (total[ph, d].T + part_up[ph, d].astype(F32)).astype(BF16)
+            part_out[ph, d] = (turned[ph, d] + part_up[ph, d].astype(F32)).astype(BF16)
 
         @pl.when(z < d)
         def _():
@@ -416,12 +420,12 @@
     def send_down(ph, d):
         @pl.when(z == LINE - 1)
         def _():
-            part_out[ph, d] = total[ph, d].T.astype(BF16)
+            part_out[ph, d] = total[d].T.astype(BF16)
 
         @pl.when((z < LINE - 1) & (z > d))
         def _():
             part_copy(ph, False, d).wait_recv()
-            part_out[ph, d] = (total[ph, d].T + part_down[ph, d].astype(F32)).astype(BF16)
+            part_out[ph, d] = (turned[ph, d] + part_down[ph, d].astype(F32)).astype(BF16)
 
         @pl.when(z > d)
         def _():
@@ -450,8 +454,8 @@
             for s in range(LINE - 1):
                 send_down(ph, s)
 
-    def finish_line(ph, out_ref):
-        final[...] = total[ph, z].T
+    def finish_line(ph):
+        final[...] = turned[ph, z]
 
         @pl.when(z > 0)
         def _():
@@ -463,7 +467,7 @@
             part_copy(ph, False, z).wait_recv()
             final[...] += part_down[ph, z].astype(F32)
 
-        out_ref[...] = final[...].astype(BF16)
+        out_ref[ph] = final[...].astype(BF16)
 
     def rest_of(q):
         full = rest_in[...].astype(F32)
@@ -507,16 +511,19 @@
     total[...] = jnp.zeros_like(total)
     combine(0, 0, planes)
     reduce_ends(0)
+    turn(0)
     lax.fori_loop(2, 3, backward_step, 0)
+    total[...] = jnp.zeros_like(total)
     combine(1, 1, planes)
     lax.fori_loop(3, planes, backward_step, 0)
     back_in[1, y] = rows_in[1, y]
     combine(1, planes, planes + 1)
     reduce_ends(1)
+    turn(1)
     reduce_line(0)
     reduce_line(1)
-    finish_line(0, moe_ref)
-    finish_line(1, gin_ref)
+    finish_line(0)
+    finish_line(1)
 
     for kind in range(3):
         hop_done(kind)
@@ -563,11 +570,11 @@
     sizes = (lax.axis_size("pipe"), planes, cap, chunk, tok, units, block)
     vmem = pl.BlockSpec(memory_space=pltpu.VMEM)
     dma = pltpu.SemaphoreType.DMA
-    moe, gin = pl.pallas_call(
+    out = pl.pallas_call(
         functools.partial(kernel, sizes),
-        out_shape=[jax.ShapeDtypeStruct((depth, tok), BF16)] * 2,
+        out_shape=jax.ShapeDtypeStruct((2, depth, tok), BF16),
         in_specs=[vmem] * 6 + [pl.BlockSpec(memory_space=pl.ANY)] * 3 + [vmem] * 2,
-        out_specs=[vmem] * 2,
+        out_specs=vmem,
         scratch_shapes=[
             pltpu.VMEM((depth, 2 * units), BF16),
             pltpu.VMEM((units, depth), BF16),
@@ -588,7 +595,8 @@
             pltpu.VMEM((2, planes, chunk, depth), BF16),
             pltpu.VMEM((2, planes, chunk, depth), BF16),
             pltpu.VMEM((2, planes, chunk, depth), BF16),
-            pltpu.VMEM((2, LINE, tok, depth), F32),
+            pltpu.VMEM((LINE, tok, depth), F32),
+            pltpu.VMEM((2, LINE, depth, tok), F32),
             pltpu.VMEM((2, LINE, depth, tok), BF16),
             pltpu.VMEM((2, LINE, depth, tok), BF16),
             pltpu.VMEM((2, LINE, depth, tok), BF16),
@@ -627,7 +635,7 @@
         saved_scales[0].T,
         saved_exponent,
     )
-    return (moe.T[None], gin.T[None])
+    return (out[0].T[None], out[1].T[None])
 
 
 def solution(mesh):

time: 254 us -> 252 us (level)
    unnamed x2 -> x0, local copies, waits for them, and re-layouts: 3.5 us -> none
where the time goes in v3:
time: 252 us; the launch traced here: 250 us
  Pallas kernels  247 us (98%)
    pallas_call x1, Pallas kernels, local(): pl.pallas_call(functools.partial(kernel, sizes), out_shape=jax.ShapeDtype...  247 us

profile of v3, /device:TPU:26, one launch (start us, length us, event | category | flops | bytes accessed | tf_op | source)
XLA Modules:
  0.0 250.4 jit_solution(10682301080395799413)
XLA Ops:
  1.3 247.1 %shard_map.122 = bf16[2,1440,128]{2,1,0:T(8,128)(2,1)} custom-call(s32[4,128]{1,0:T(4,128)} %bitcast.44, f32[4,128]{1,0:T(4,128)} %bitcast.45, s32[4,128]{1,0:T(4,128)} %bitcast.46, f32[4,128]{1,0:T(4,128)} %bitcast.47, bf16[1440,128]{1,0:T(8,128)(2,1)} %bitcast.41, bf16[1440,128]{1,0:T(8,128)(2,1)} %bitcast.42, bf16[1440,1440]{1,0:T(8,128)(2,1)} %bitcast.38, ...), custom_call_target="tpu_custom_call" | custom-call | flops 27072921600 | bytes 16777216 | tf_op jit(solution)/shard_map/pallas_call | solution.py:573
  248.4 2.0 slice_bitcast_fusion

commit v4 on v3

--- a/solution.py
+++ b/solution.py
@@ -242,6 +242,11 @@
     hop(0, 2)
     hop(2, 3)
 
+    @pl.when(ends)
+    def _():
+        rest_copy.start()
+        coef_start(0)
+
     plane_expert = (
         2 * lax.broadcasted_iota(jnp.int32, (8, tok), 0) + z // 2
     ).astype(F32)
@@ -322,8 +327,6 @@
 
     @pl.when(ends)
     def _():
-        rest_copy.start()
-        coef_start(0)
         coef_start(1)
 
     hop(1, 1)

time: 252 us -> 261 us (1.036)
  Pallas kernels: 247 us -> 258 us
    pallas_call x1, Pallas kernels: 247 us -> 258 us  [local(): pl.pallas_call(functools.partial(kernel, sizes), out_shape=jax.ShapeDtype...]
where the time goes in v4:
time: 261 us
  Pallas kernels  258 us (99%)
    pallas_call x1, Pallas kernels, local(): pl.pallas_call(functools.partial(kernel, sizes), out_shape=jax.ShapeDtype...  258 us

profile of v4, /device:TPU:26, one launch (start us, length us, event | category | flops | bytes accessed | tf_op | source)
XLA Modules:
  0.0 260.9 jit_solution(10131540609736544050)
XLA Ops:
  1.3 257.6 %shard_map.122 = bf16[2,1440,128]{2,1,0:T(8,128)(2,1)} custom-call(s32[4,128]{1,0:T(4,128)} %bitcast.44, f32[4,128]{1,0:T(4,128)} %bitcast.45, s32[4,128]{1,0:T(4,128)} %bitcast.46, f32[4,128]{1,0:T(4,128)} %bitcast.47, bf16[1440,128]{1,0:T(8,128)(2,1)} %bitcast.41, bf16[1440,128]{1,0:T(8,128)(2,1)} %bitcast.42, bf16[1440,1440]{1,0:T(8,128)(2,1)} %bitcast.38, ...), custom_call_target="tpu_custom_call" | custom-call | flops 27072921600 | bytes 16777216 | tf_op jit(solution)/shard_map/pallas_call | solution.py:576
  258.9 2.0 slice_bitcast_fusion
